TPU v7x, 256 devices: a whole 4x4x8 slice. The times are simulated.
256 devices in a mesh: outer: 8 (over y, x_hi), fsdp: 8 (over z), tp: 4 (over x_lo, core).
Axes of the slice: x: 4 (x_hi: 2, x_lo: 2; x = x_hi * 2 + x_lo), y: 4, z: 8, core: 2. Of those that a mesh axis runs over, the one named last changes fastest.
Arguments:
- pseudo_grad: float32 [8, 512, 12288], P('outer', 'fsdp', 'tp'), may hold values from -6 to 6
- outer_params: float32 [512, 12288], P('fsdp', 'tp'), may hold values from -6 to 6
- momentum: float32 [512, 12288], P('fsdp', 'tp'), may hold values from -6 to 6
- hidden: bfloat16 [8, 3072, 12288], P('outer', 'fsdp', 'tp'), may hold values from -6 to 6
- kv_weight: bfloat16 [8, 12288, 1024], P('outer', 'fsdp', 'tp'), may hold values from -0.0546875 to 0.0546875
- kv_cotangent: bfloat16 [8, 3072, 1024], P('outer', 'fsdp', 'tp'), may hold values from -4 to 4
Outputs:
- new_params: float32 [512, 12288], P('fsdp', 'tp')
- new_momentum: float32 [512, 12288], P('fsdp', 'tp')
- keys_values: bfloat16 [8, 3072, 1024], P('outer', 'fsdp', 'tp')
- input_grad: bfloat16 [8, 3072, 12288], P('outer', 'fsdp', 'tp')
- weight_grad: bfloat16 [8, 12288, 1024], P('outer', 'fsdp', 'tp')
All inputs are finite; a program needn't handle non-finite values.
Results may differ from a plain program's by a relative error of at most 0.017.
Values may be sent and summed in bfloat16 or wider, within the bound.
A program may use at most 128 MiB of HBM per device.

v0:
```python
import jax
import jax.numpy as jnp
from jax import lax
from jax.sharding import PartitionSpec as P

outer_beta = 0.9
outer_rate = 0.7


def nesterov(average, params_old, moment_old):
    moment_new = outer_beta * moment_old + average
    params_new = params_old - outer_rate * (average + outer_beta * moment_new)
    return (params_new, moment_new)


def per_device(pseudo_grad, outer_params, momentum, hidden, kv_weight, kv_cotangent):
    tokens = hidden[0]
    weights = kv_weight[0]
    cotangent = kv_cotangent[0]
    full_tokens = lax.all_gather(tokens, "tp", axis=1, tiled=True)
    piece = lax.all_gather(weights, "fsdp", axis=0, tiled=True)
    feature_block = full_tokens
    running = jnp.dot(feature_block, piece, preferred_element_type=jnp.float32)
    keys_values = running.astype(jnp.bfloat16)[None]
    feature_block = full_tokens
    weight_rows = lax.psum_scatter(
        lax.dot_general(
            feature_block, cotangent, (((0,), (0,)), ((), ())), preferred_element_type=jnp.float32
        ).astype(jnp.bfloat16),
        "fsdp",
        scatter_dimension=0,
        tiled=True,
    )
    weight_grad = weight_rows[None]
    input_rows = lax.psum_scatter(
        lax.dot_general(
            piece, cotangent, (((1,), (1,)), ((), ())), preferred_element_type=jnp.float32
        ).astype(jnp.bfloat16),
        "tp",
        scatter_dimension=0,
        tiled=True,
    ).astype(jnp.float32)
    input_grad = input_rows.T.astype(jnp.bfloat16)[None]
    slab_block = pseudo_grad[0]
    pods = lax.axis_size("outer")
    average = lax.psum(slab_block.astype(jnp.bfloat16), "outer").astype(jnp.float32) / pods
    new_params, new_momentum = nesterov(average, outer_params, momentum)
    return (new_params, new_momentum, keys_values, input_grad, weight_grad)


def solution(mesh):
    return jax.shard_map(
        per_device,
        mesh=mesh,
        in_specs=(
            P("outer", "fsdp", "tp"),
            P("fsdp", "tp"),
            P("fsdp", "tp"),
            P("outer", "fsdp", "tp"),
            P("outer", "fsdp", "tp"),
            P("outer", "fsdp", "tp"),
        ),
        out_specs=(
            P("fsdp", "tp"),
            P("fsdp", "tp"),
            P("outer", "fsdp", "tp"),
            P("outer", "fsdp", "tp"),
            P("outer", "fsdp", "tp"),
        ),
        check_vma=False,
    )
```

profile of v0, /device:TPU:1, one launch (start us, length us, event | category | flops | bytes accessed | tf_op | source)
XLA Modules:
  0.0 362.6 jit_solution(6066419222137994193)
XLA Ops:
  8.0 0.0 copy-start
  8.0 0.0 all-gather.7.cloned.1.call-start
  8.1 0.7 all-gather.7.cloned.1.call-update
  8.7 0.0 all-gather.5.cloned.1.call-start
  8.8 0.7 all-gather.5.cloned.1.call-update
  9.5 0.0 all-reduce.2.cloned.1.call-start
  9.5 1.9 convert_bitcast_fusion
  11.5 0.0 all-reduce.2.cloned.1.call-update
  11.5 0.0 reduce-scatter.3.cloned.1.call-start
  11.5 77.5 %all-gather.7.cloned.1.call-done = bf16[1,12288,256]{2,1,0:T(8,128)(2,1)} async-done(((bf16[1,1536,256]{2,1,0:T(8,128)(2,1)}), bf16[1,12288,256]{2,1,0:T(8,128)(2,1)}) %all-gather.7.cloned.1.call-update) | async-done | bytes 6291472 | tf_op jit(solution)/shard_map/all_gather | solution.py:21
  89.1 0.0 copy-done
  89.1 9.9 %convolution_convert_fusion = bf16[12288,384]{1,0:T(8,128)(2,1)} fusion(bf16[1,12288,256]{2,1,0:T(8,128)(2,1)} %all-gather.7.cloned.1.call-done, bf16[1,384,256]{2,1,0:T(8,128)(2,1)S(1)} %copy-done), kind=kOutput, calls=%fused_computation | convolution fusion | flops 2420637696 | bytes 15925248 | tf_op jit(solution)/shard_map/dot_general | solution.py:36
  99.0 0.0 reduce-scatter.3.cloned.1.call-update
  99.0 0.0 reduce-scatter.5.cloned.1.call-start
  99.1 83.7 %all-gather.5.cloned.1.call-done = bf16[1,384,12288]{2,1,0:T(8,128)(2,1)} async-done(((bf16[1,384,3072]{2,1,0:T(8,128)(2,1)}), bf16[1,384,12288]{2,1,0:T(8,128)(2,1)}) %all-gather.5.cloned.1.call-update) | async-done | bytes 9437200 | tf_op jit(solution)/shard_map/all_gather | solution.py:20
  182.7 9.9 %convolution_convert_fusion.1 = bf16[12288,256]{1,0:T(8,128)(2,1)} fusion(bf16[1,384,12288]{2,1,0:T(8,128)(2,1)} %all-gather.5.cloned.1.call-done, bf16[1,384,256]{2,1,0:T(8,128)(2,1)S(1)} %copy-done), kind=kOutput, calls=%fused_computation.1 | convolution fusion | flops 2419064832 | bytes 15925248 | tf_op jit(solution)/shard_map/dot_general | solution.py:27
  192.6 0.0 copy-start.1
  192.6 0.0 copy-start.2
  192.6 0.0 reduce-scatter.5.cloned.1.call-update
  192.6 0.0 all-reduce.2.cloned.1.call-done
  192.7 1.1 copy-done.1
  193.7 0.2 copy-done.2
  194.0 2.3 multiply_subtract_fusion
  196.3 9.6 %fusion.10 = bf16[1,384,256]{2,1,0:T(8,128)(2,1)} fusion(bf16[1,12288,256]{2,1,0:T(8,128)(2,1)} %all-gather.7.cloned.1.call-done, bf16[1,384,12288]{2,1,0:T(8,128)(2,1)} %all-gather.5.cloned.1.call-done), kind=kOutput, calls=%fused_computation.8 | convolution fusion | flops 2416017408 | bytes 15925248 | tf_op jit(solution)/shard_map/dot_general | solution.py:23
  205.9 70.5 %reduce-scatter.3.cloned.1.call-done = bf16[3072,384]{1,0:T(8,128)(2,1)} async-done(((bf16[12288,384]{1,0:T(8,128)(2,1)}), bf16[3072,384]{1,0:T(8,128)(2,1)}) %reduce-scatter.3.cloned.1.call-update) | async-done | bytes 2359312 | tf_op jit(solution)/shard_map/reduce_scatter | solution.py:35
  276.4 4.3 %copy.11 = bf16[1,384,3072]{2,1,0:T(8,128)(2,1)} copy(bf16[1,384,3072]{1,2,0:T(8,128)(2,1)} %bitcast.31) | data formatting | bytes 4718592
  280.7 74.8 %reduce-scatter.5.cloned.1.call-done = bf16[1536,256]{1,0:T(8,128)(2,1)} async-done(((bf16[12288,256]{1,0:T(8,128)(2,1)}), bf16[1536,256]{1,0:T(8,128)(2,1)}) %reduce-scatter.5.cloned.1.call-update) | async-done | bytes 786448 | tf_op jit(solution)/shard_map/reduce_scatter | solution.py:26
Async XLA Ops:
  8.0 81.1 %copy-start = (bf16[1,384,256]{2,1,0:T(8,128)(2,1)S(1)}, bf16[1,384,256]{2,1,0:T(8,128)(2,1)}, u32[]{:S(2)}) copy-start(bf16[1,384,256]{2,1,0:T(8,128)(2,1)} %param.11) | copy-start | bytes 589828
  8.0 81.1 %all-gather.7.cloned.1.call-start = ((), (), s32[]{:S(2)}) async-start(), calls=%async_computation.6 | async-start | bytes 7077888 | tf_op jit(solution)/shard_map/all_gather | solution.py:21
  8.7 174.0 %all-gather.5.cloned.1.call-start = ((), (), s32[]{:S(2)}) async-start(), calls=%async_computation.5 | async-start | bytes 11796480 | tf_op jit(solution)/shard_map/all_gather | solution.py:20
  9.5 183.2 %all-reduce.2.cloned.1.call-start = ((), (), s32[]{:S(2)}) async-start(), calls=%async_computation.2 | async-start | bytes 786432 | tf_op jit(solution)/shard_map/psum | solution.py:46
  11.5 264.9 %reduce-scatter.3.cloned.1.call-start = ((), (), s32[]{:S(2)}) async-start(), calls=%async_computation.3 | async-start | bytes 11796480 | tf_op jit(solution)/shard_map/reduce_scatter | solution.py:35
  99.0 256.4 %reduce-scatter.5.cloned.1.call-start = ((), (), s32[]{:S(2)}) async-start(), calls=%async_computation.4 | async-start | bytes 7077888 | tf_op jit(solution)/shard_map/reduce_scatter | solution.py:26
  192.6 1.1 copy-start.1
  192.6 1.4 copy-start.2
Sparse Core Ops, SparseCore 0:
  10.8 78.2 all-gather.6
  91.0 91.6 all-gather.4
  185.5 90.8 reduce-scatter.2
  279.6 75.8 reduce-scatter.4
Sparse Core Ops, SparseCore 1:
  13.2 88.6 all-reduce.1
where the time goes:
time: 363 us
  waiting for transfers between devices  308 us (85%)
  matrix products  29.4 us (8%)
  between operations  15.2 us (4%)
  local copies, waits for them, and re-layouts  5.59 us (2%)
  other arithmetic  4.26 us (1%)
    all_gather x1, waiting for transfers between devices, per_device(): full_tokens = lax.all_gather(tokens, 'tp', axis=1, tiled=True)  83.7 us
    all_gather x1, waiting for transfers between devices, per_device(): piece = lax.all_gather(weights, 'fsdp', axis=0, tiled=True)  77.5 us
    reduce_scatter x1, waiting for transfers between devices, per_device(): lax.psum_scatter(lax.dot_general(feature_block, cotangent, (((0,), (0,)),...  74.8 us
    reduce_scatter x1, waiting for transfers between devices, per_device(): lax.psum_scatter(lax.dot_general(piece, cotangent, (((1,), (1,)), ((), ()...  70.5 us
    dot_general x1, matrix products, per_device(): lax.dot_general(piece, cotangent, (((1,), (1,)), ((), ())), preferred_ele...  9.91 us
    dot_general x1, matrix products, per_device(): lax.dot_general(feature_block, cotangent, (((0,), (0,)), ((), ())), prefe...  9.86 us
    dot_general x1, matrix products, per_device(): running = jnp.dot(feature_block, piece, preferred_element_type=jnp.float32)  9.62 us
  transfers between devices with their start and end apart: 5, of which 4 were waited for; matrix products, arithmetic and copies ran while one was open for 10% of the time, Pallas kernels for 0%

commit v1 on v0

v1 whole, which is shorter than its diff:
```python
import functools

import jax
import jax.numpy as jnp
from jax import lax
from jax.experimental import pallas as pl
from jax.experimental.pallas import tpu as pltpu
from jax.sharding import PartitionSpec as P

outer_beta = 0.9
outer_rate = 0.7
MESH = pl.DeviceIdType.MESH
BF = jnp.bfloat16
F32 = jnp.float32

Z = 8
PIECES = 16
STEPS = 7


def nesterov(average, params_old, moment_old):
    moment_new = outer_beta * moment_old + average
    params_new = params_old - outer_rate * (average + outer_beta * moment_new)
    return (params_new, moment_new)


def kernel(
    hid_in, w_in, cot_in,
    kv_out, ig_out, wg_out,
    hid, wfull, cot, cot_t, part, sib, far, rs_out, rs_in, kv_acc, kv_stage, ig_stage, wg_stage,
    load_sem, store_sem,
    ag_send, ag_recv, rs_send, rs_recv,
    hx_send, hx_recv, hs_send, hs_recv, hf_send, hf_recv,
    p_send, p_recv, s_send, s_recv,
):
    z = lax.axis_index("fsdp")
    t = lax.axis_index("tp")
    x = t // 2
    c = lax.rem(t, 2)
    sibling = 2 * x + (1 - c)
    peer = 2 * (1 - x) + c
    up = lax.rem(z + 1, Z)
    down = lax.rem(z + Z - 1, Z)
    half = w_in.shape[0] // 2

    def remote(src, dst, send, recv, where):
        return pltpu.make_async_remote_copy(
            src_ref=src, dst_ref=dst, send_sem=send, recv_sem=recv, device_id=where, device_id_type=MESH
        )

    barrier = pltpu.get_barrier_semaphore()
    for where in ({"fsdp": up}, {"fsdp": down}, {"tp": sibling}, {"tp": peer}):
        pl.semaphore_signal(barrier, inc=1, device_id=where, device_id_type=MESH)
    pl.semaphore_wait(barrier, 4)

    def ring(block):
        return lax.rem(block + 2 * Z, Z)

    def ag_piece(j, direction, at):
        if direction == 0:
            return 2 * ring(at - j // 2) + lax.rem(j, 2)
        return 2 * ring(at + j // 2) + 1 - lax.rem(j, 2)

    def ag_copy(j, direction):
        b = ag_piece(j, direction, z)
        return remote(
            wfull.at[b], wfull.at[b], ag_send.at[direction, j], ag_recv.at[direction, j],
            {"fsdp": up if direction == 0 else down},
        )

    def ag_first(j, direction):
        h = j if direction == 0 else 1 - j
        return remote(
            w_in.at[pl.ds(h * half, half)], wfull.at[2 * z + h], ag_send.at[direction, j], ag_recv.at[direction, j],
            {"fsdp": up if direction == 0 else down},
        )

    for j in range(2):
        for direction in range(2):
            ag_first(j, direction).start()

    def hid_view(k):
        return hid_in.at[:, pl.ds(k * half, half)]

    def hx_copy(k):
        return remote(hid_view(k), hid.at[4 * t + k], hx_send.at[k], hx_recv.at[k], {"tp": peer})

    def hs_copy(k):
        return remote(hid_view(k), hid.at[4 * t + k], hs_send.at[k], hs_recv.at[k], {"tp": sibling})

    def hf_copy(k):
        return remote(hid.at[4 * peer + k], hid.at[4 * peer + k], hf_send.at[k], hf_recv.at[k], {"tp": sibling})

    for k in range(4):
        hx_copy(k).start()
    loads = [pltpu.make_async_copy(cot_in, cot, load_sem.at[0])]
    for h in range(2):
        loads.append(pltpu.make_async_copy(w_in.at[pl.ds(h * half, half)], wfull.at[2 * z + h], load_sem.at[1 + h]))
    for k in range(4):
        loads.append(pltpu.make_async_copy(hid_view(k), hid.at[4 * t + k], load_sem.at[3 + k]))
    for copy in loads:
        copy.start()
    for k in range(4):
        hs_copy(k).start()
    for copy in loads:
        copy.wait()
    cot_t[...] = cot[...].astype(F32).T.astype(BF)

    def column_part(b):
        part[b] = lax.dot_general(
            cot[...], wfull[b], (((1,), (1,)), ((), ())), preferred_element_type=F32
        ).astype(BF)

    def slot_of(b):
        return 4 * (b // 8) + lax.rem(b, 4)

    def owner_core(b):
        return lax.rem(b // 4, 2)

    def p_copy(b):
        s = slot_of(b)
        return remote(part.at[b], sib.at[s], p_send.at[s], p_recv.at[s], {"tp": sibling})

    def s_copy(b):
        k = lax.rem(b, 4)
        return remote(part.at[b], far.at[k], s_send.at[k], s_recv.at[k], {"tp": peer})

    def make_part(b):
        column_part(b)

        @pl.when(owner_core(b) != c)
        def _():
            p_copy(b).start()

    def pair_part(b):
        @pl.when((owner_core(b) == c) & (b // 8 != x))
        def _():
            p_copy(b).wait_recv()
            part[b] = (part[b].astype(F32) + sib[slot_of(b)].astype(F32)).astype(BF)
            s_copy(b).start()

    make_part(2 * z)
    make_part(2 * z + 1)
    pair_part(2 * z)
    pair_part(2 * z + 1)

    def ag_step(j, carry):
        for direction in range(2):
            ag_copy(j, direction).wait_recv()

            @pl.when(j + 2 < STEPS)
            def _():
                ag_copy(j + 2, direction).start()

        here_up = ag_piece(j, 0, z - 1)
        here_down = ag_piece(j, 1, z + 1)
        make_part(here_up)
        make_part(here_down)
        for at, k in ((1, 0), (3, 1), (4, 2), (6, 3)):
            @pl.when(j == at)
            def _():
                hx_copy(k).wait_recv()
                hf_copy(k).start()
        pair_part(here_up)
        pair_part(here_down)
        return carry

    lax.fori_loop(0, STEPS, ag_step, 0)

    for k in range(4):
        hs_copy(k).wait_recv()
        hf_copy(k).wait_recv()

    def rs_piece(j, direction):
        if direction == 0:
            return 2 * ring(z + 4 - (j + 1) // 2) + lax.rem(j, 2)
        return 2 * ring(z - 4 + (j + 1) // 2) + 1 - lax.rem(j, 2)

    def rs_copy(j, direction):
        return remote(
            rs_out.at[direction, j], rs_in.at[direction, j], rs_send.at[direction, j], rs_recv.at[direction, j],
            {"fsdp": up if direction == 0 else down},
        )

    def token_sum(b):
        return jnp.dot(cot_t[...], hid[b], preferred_element_type=F32)

    for j in range(2):
        for direction in range(2):
            rs_out[direction, j] = token_sum(rs_piece(j, direction)).astype(BF)
            rs_copy(j, direction).start()

    kv_acc[...] = jnp.zeros_like(kv_acc)

    def rs_step(j, carry):
        for direction in range(2):
            mine = token_sum(rs_piece(j, direction))
            rs_copy(j - 2, direction).wait_recv()
            rs_out[direction, j] = (mine + rs_in[direction, j - 2].astype(F32)).astype(BF)
            rs_copy(j, direction).start()
        for i in range(3):
            b = 3 * (j - 2) + i
            kv_acc[...] += jnp.dot(hid[b], wfull[b], preferred_element_type=F32)
        return carry

    lax.fori_loop(2, STEPS, rs_step, 0)
    kv_stage[...] = (kv_acc[...] + jnp.dot(hid[15], wfull[15], preferred_element_type=F32)).astype(BF)
    stores = [pltpu.make_async_copy(kv_stage, kv_out, store_sem.at[0])]
    stores[0].start()

    for k in range(4):
        b = 4 * t + k
        p_copy(b).wait_recv()
        s_copy(b).wait_recv()
        total = part[b].astype(F32) + sib[4 * x + k].astype(F32) + far[k].astype(F32)
        ig_stage[k] = total.astype(BF)
        stores.append(pltpu.make_async_copy(ig_stage.at[k], ig_out.at[:, pl.ds(k * half, half)], store_sem.at[1 + k]))
        stores[-1].start()

    for direction in range(2):
        rs_copy(5, direction).wait_recv()
    for direction in range(2):
        rs_copy(6, direction).wait_recv()
    for h in range(2):
        total = token_sum(2 * z + h) + rs_in[0, 6 - h].astype(F32) + rs_in[1, 5 + h].astype(F32)
        wg_stage[pl.ds(h * half, half)] = total.T.astype(BF)
        stores.append(
            pltpu.make_async_copy(
                wg_stage.at[pl.ds(h * half, half)], wg_out.at[pl.ds(h * half, half)], store_sem.at[5 + h]
            )
        )
        stores[-1].start()

    for j in range(STEPS):
        for direction in range(2):
            ag_copy(j, direction).wait_send()
            rs_copy(j, direction).wait_send()
    for k in range(4):
        hx_copy(k).wait_send()
        hs_copy(k).wait_send()
        hf_copy(k).wait_send()
        s_copy(4 * peer + k).wait_send()
        p_copy(4 * sibling + k).wait_send()
        p_copy(4 * (3 - t) + k).wait_send()
    for copy in stores:
        copy.wait()


def inner(hidden, weights, cotangent):
    tokens, width = hidden.shape
    rows, cols = weights.shape
    half = rows // 2
    sems = pltpu.SemaphoreType.DMA
    any_spec = pl.BlockSpec(memory_space=pl.ANY)
    return pl.pallas_call(
        kernel,
        out_shape=(
            jax.ShapeDtypeStruct((tokens, cols), BF),
            jax.ShapeDtypeStruct((tokens, width), BF),
            jax.ShapeDtypeStruct((rows, cols), BF),
        ),
        in_specs=[any_spec] * 3,
        out_specs=[any_spec] * 3,
        scratch_shapes=[
            pltpu.VMEM((PIECES, tokens, half), BF),
            pltpu.VMEM((PIECES, half, cols), BF),
            pltpu.VMEM((tokens, cols), BF),
            pltpu.VMEM((cols, tokens), BF),
            pltpu.VMEM((PIECES, tokens, half), BF),
            pltpu.VMEM((8, tokens, half), BF),
            pltpu.VMEM((4, tokens, half), BF),
            pltpu.VMEM((2, STEPS, cols, half), BF),
            pltpu.VMEM((2, STEPS, cols, half), BF),
            pltpu.VMEM((tokens, cols), F32),
            pltpu.VMEM((tokens, cols), BF),
            pltpu.VMEM((4, tokens, half), BF),
            pltpu.VMEM((rows, cols), BF),
            sems((7,)), sems((7,)),
            sems((2, STEPS)), sems((2, STEPS)), sems((2, STEPS)), sems((2, STEPS)),
            sems((4,)), sems((4,)), sems((4,)), sems((4,)), sems((4,)), sems((4,)),
            sems((8,)), sems((8,)), sems((4,)), sems((4,)),
        ],
        compiler_params=pltpu.CompilerParams(
            collective_id=0, has_side_effects=True, vmem_limit_bytes=60 * 1024 * 1024
        ),
        cost_estimate=pl.CostEstimate(flops=7_250_000_000, bytes_accessed=8_000_000, transcendentals=0),
        name="inner_step",
    )(hidden, weights, cotangent)


def per_device(pseudo_grad, outer_params, momentum, hidden, kv_weight, kv_cotangent):
    keys_values, input_grad, weight_grad = inner(hidden[0], kv_weight[0], kv_cotangent[0])
    pods = lax.axis_size("outer")
    average = lax.psum(pseudo_grad[0].astype(BF), "outer").astype(F32) / pods
    new_params, new_momentum = nesterov(average, outer_params, momentum)
    return (new_params, new_momentum, keys_values[None], input_grad[None], weight_grad[None])


def solution(mesh):
    return jax.shard_map(
        per_device,
        mesh=mesh,
        in_specs=(
            P("outer", "fsdp", "tp"),
            P("fsdp", "tp"),
            P("fsdp", "tp"),
            P("outer", "fsdp", "tp"),
            P("outer", "fsdp", "tp"),
            P("outer", "fsdp", "tp"),
        ),
        out_specs=(
            P("fsdp", "tp"),
            P("fsdp", "tp"),
            P("outer", "fsdp", "tp"),
            P("outer", "fsdp", "tp"),
            P("outer", "fsdp", "tp"),
        ),
        check_vma=False,
    )
```

time: 363 us -> 157 us (0.43)
  waiting for transfers between devices: 308 us -> 0.04 us
  Pallas kernels: 0 us -> 135 us
  matrix products: 29.4 us -> 0 us
    all_gather x2 -> x0, waiting for transfers between devices: 161 us -> none  [the longest x1 83.7 us: per_device(): full_tokens = lax.all_gather(tokens, 'tp', axis=1, tiled=True)]
    reduce_scatter x2 -> x0, waiting for transfers between devices: 145 us -> none  [the longest x1 74.8 us: per_device(): lax.psum_scatter(lax.dot_general(feature_block, cotangent, (((0,), (0,)),...]
    pallas_call x0 -> x1, Pallas kernels: none -> 135 us  [inner(): pl.pallas_call(kernel, out_shape=(jax.ShapeDtypeStruct((tokens, cols), BF...]
    dot_general x3 -> x0, matrix products: 29.4 us -> none  [the longest x1 9.91 us: per_device(): lax.dot_general(piece, cotangent, (((1,), (1,)), ((), ())), preferred_ele...]
  transfers between devices with their start and end apart: 5 -> 1, of which waited for: 4 -> 0; matrix products, arithmetic and copies ran while one was open for 10% -> 0% of each run, Pallas kernels for 0% -> 86%
where the time goes in v1:
time: 157 us
  Pallas kernels  135 us (86%)
  between operations  14.1 us (9%)
  other arithmetic  4.67 us (3%)
  local copies, waits for them, and re-layouts  3.25 us (2%)
    pallas_call x1, Pallas kernels, inner(): pl.pallas_call(kernel, out_shape=(jax.ShapeDtypeStruct((tokens, cols), BF...  135 us
    unnamed x11, local copies, waits for them, and re-layouts  3.25 us
  transfers between devices with their start and end apart: 1, of which 0 were waited for; matrix products, arithmetic and copies ran while one was open for 0% of the time, Pallas kernels for 86%

profile of v1, /device:TPU:1, one launch (start us, length us, event | category | flops | bytes accessed | tf_op | source)
XLA Modules:
  0.0 156.7 jit_solution(11758310982511840181)
XLA Ops:
  7.2 0.0 all-reduce.2.cloned.1.call-start
  7.2 1.9 %convert_bitcast_fusion = bf16[64,3072]{1,0:T(8,128)(2,1)} fusion(f32[1,64,3072]{2,1,0:T(8,128)} %param.6), kind=kLoop, calls=%fused_computation.3 | loop fusion | flops 196608 | bytes 1179648 | tf_op jit(solution)/shard_map/convert_element_type | solution.py:294
  9.1 0.0 all-reduce.2.cloned.1.call-update
  9.2 0.0 copy-start.1
  9.2 134.6 %inner_step.1 = (bf16[384,256]{1,0:T(8,128)(2,1)}, bf16[384,3072]{1,0:T(8,128)(2,1)}, bf16[1536,256]{1,0:T(8,128)(2,1)}) custom-call(bf16[384,3072]{1,0:T(8,128)(2,1)} %bitcast.11, bf16[1536,256]{1,0:T(8,128)(2,1)} %bitcast.12, bf16[384,256]{1,0:T(8,128)(2,1)} %bitcast.13), custom_call_target="tpu_custom_call" | custom-call | flops 7249999872 | bytes 8000000 | tf_op jit(solution)/shard_map/inner_step/pallas_call | solution.py:255
  143.8 0.0 copy-start.3
  143.8 0.0 copy-start
  143.8 0.0 all-reduce.2.cloned.1.call-done
  143.8 0.0 copy-done.1
  143.9 2.7 %multiply_subtract_fusion = (f32[64,3072]{1,0:T(8,128)}, f32[64,3072]{1,0:T(8,128)}) fusion(f32[64,3072]{1,0:T(8,128)S(1)} %copy-done.1, bf16[64,3072]{1,0:T(8,128)(2,1)} %all-reduce.2.cloned.1.call-done, f32[64,3072]{1,0:T(8,128)} %param.8), kind=kLoop, calls=%fused_computation | loop fusion | flops 1572864 | bytes 3538944 | tf_op jit(solution)/shard_map/sub | solution.py:23
  146.6 0.0 copy-done.3
  146.6 0.7 copy.15
  147.3 0.0 copy-done
  147.3 0.0 copy-start.2
  147.3 1.4 copy.16
  148.7 0.3 copy-done.2
  149.0 0.9 copy.17
Async XLA Ops:
  7.2 136.7 %all-reduce.2.cloned.1.call-start = ((), (), s32[]{:S(2)}) async-start(), calls=%async_computation | async-start | bytes 786432 | tf_op jit(solution)/shard_map/psum | solution.py:294
  9.2 134.7 %copy-start.1 = (f32[64,3072]{1,0:T(8,128)S(1)}, f32[64,3072]{1,0:T(8,128)}, u32[]{:S(2)}) copy-start(f32[64,3072]{1,0:T(8,128)} %param.7) | copy-start | bytes 2359300
  143.8 2.8 %copy-start.3 = (bf16[384,256]{1,0:T(8,128)(2,1)S(1)}, bf16[384,256]{1,0:T(8,128)(2,1)}, u32[]{:S(2)}) copy-start(bf16[384,256]{1,0:T(8,128)(2,1)} %get-tuple-element.8) | copy-start | bytes 589828
  143.8 3.5 %copy-start = (bf16[384,3072]{1,0:T(8,128)(2,1)S(1)}, bf16[384,3072]{1,0:T(8,128)(2,1)}, u32[]{:S(2)}) copy-start(bf16[384,3072]{1,0:T(8,128)(2,1)} %get-tuple-element.9) | copy-start | bytes 7077892
  147.3 1.7 %copy-start.2 = (bf16[1536,256]{1,0:T(8,128)(2,1)S(1)}, bf16[1536,256]{1,0:T(8,128)(2,1)}, u32[]{:S(2)}) copy-start(bf16[1536,256]{1,0:T(8,128)(2,1)} %get-tuple-element.10) | copy-start | bytes 2359300
Sparse Core Ops, SparseCore 0:
  11.2 94.6 all-reduce.1

commit v2 on v1

--- a/solution.py
+++ b/solution.py
@@ -1,5 +1,3 @@
-import functools
-
 import jax
 import jax.numpy as jnp
 from jax import lax
@@ -14,6 +12,7 @@
 F32 = jnp.float32
 
 Z = 8
+Y = 4
 PIECES = 16
 STEPS = 7
 
@@ -25,23 +24,32 @@
 
 
 def kernel(
-    hid_in, w_in, cot_in,
-    kv_out, ig_out, wg_out,
+    pg_in, par_in, mom_in, hid_in, w_in, cot_in,
+    par_out, mom_out, kv_out, ig_out, wg_out,
     hid, wfull, cot, cot_t, part, sib, far, rs_out, rs_in, kv_acc, kv_stage, ig_stage, wg_stage,
+    pg, par, mom, y_out, y_in, pod_out, pod_in, avg,
     load_sem, store_sem,
     ag_send, ag_recv, rs_send, rs_recv,
-    hx_send, hx_recv, hs_send, hs_recv, hf_send, hf_recv,
+    hx_send, hx_recv, hs_send, hs_recv,
     p_send, p_recv, s_send, s_recv,
+    y_send, y_recv, v_send, v_recv, pod_send, pod_recv,
 ):
+    o = lax.axis_index("outer")
     z = lax.axis_index("fsdp")
     t = lax.axis_index("tp")
     x = t // 2
     c = lax.rem(t, 2)
     sibling = 2 * x + (1 - c)
     peer = 2 * (1 - x) + c
+    diagonal = 3 - t
     up = lax.rem(z + 1, Z)
     down = lax.rem(z + Z - 1, Z)
+    y = o // 2
+    x_hi = lax.rem(o, 2)
+    other_hi = 2 * y + 1 - x_hi
+    y_at = [lax.rem(y + i, Y) for i in range(Y)]
     half = w_in.shape[0] // 2
+    quarter = pg_in.shape[1] // Y
 
     def remote(src, dst, send, recv, where):
         return pltpu.make_async_remote_copy(
@@ -49,9 +57,11 @@
         )
 
     barrier = pltpu.get_barrier_semaphore()
-    for where in ({"fsdp": up}, {"fsdp": down}, {"tp": sibling}, {"tp": peer}):
+    partners = [{"fsdp": up}, {"fsdp": down}, {"tp": sibling}, {"tp": peer}, {"outer": other_hi}]
+    partners += [{"outer": 2 * y_at[i] + x_hi} for i in range(1, Y)]
+    for where in partners:
         pl.semaphore_signal(barrier, inc=1, device_id=where, device_id_type=MESH)
-    pl.semaphore_wait(barrier, 4)
+    pl.semaphore_wait(barrier, len(partners))
 
     def ring(block):
         return lax.rem(block + 2 * Z, Z)
@@ -79,25 +89,40 @@
         for direction in range(2):
             ag_first(j, direction).start()
 
+    def farther(of):
+        low = ring(2 * of - z)
+        high = ring(2 * of + 1 - z)
+        return (jnp.minimum(high, Z - high) > jnp.minimum(low, Z - low)).astype(jnp.int32)
+
+    def hid_turn(i, of):
+        first = farther(of)
+        return 2 * lax.rem(first + i // 2, 2) + i % 2
+
     def hid_view(k):
-        return hid_in.at[:, pl.ds(k * half, half)]
-
-    def hx_copy(k):
-        return remote(hid_view(k), hid.at[4 * t + k], hx_send.at[k], hx_recv.at[k], {"tp": peer})
+        return hid_in.at[:, pl.ds(pl.multiple_of(k * half, half), half)]
+
+    def hx_copy(i):
+        k = hid_turn(i, t)
+        return remote(hid_view(k), hid.at[4 * t + k], hx_send.at[i], hx_recv.at[i], {"tp": peer})
 
     def hs_copy(k):
-        return remote(hid_view(k), hid.at[4 * t + k], hs_send.at[k], hs_recv.at[k], {"tp": sibling})
-
-    def hf_copy(k):
-        return remote(hid.at[4 * peer + k], hid.at[4 * peer + k], hf_send.at[k], hf_recv.at[k], {"tp": sibling})
-
-    for k in range(4):
-        hx_copy(k).start()
+        b = 4 * t + k
+        return remote(hid_view(k), hid.at[b], hs_send.at[k], hs_recv.at[b], {"tp": sibling})
+
+    def hf_copy(i):
+        b = 4 * peer + hid_turn(i, peer)
+        return remote(hid.at[b], hid.at[b], hs_send.at[4 + i], hs_recv.at[b], {"tp": sibling})
+
+    for i in range(4):
+        hx_copy(i).start()
     loads = [pltpu.make_async_copy(cot_in, cot, load_sem.at[0])]
     for h in range(2):
         loads.append(pltpu.make_async_copy(w_in.at[pl.ds(h * half, half)], wfull.at[2 * z + h], load_sem.at[1 + h]))
     for k in range(4):
         loads.append(pltpu.make_async_copy(hid_view(k), hid.at[4 * t + k], load_sem.at[3 + k]))
+    loads.append(pltpu.make_async_copy(pg_in, pg, load_sem.at[7]))
+    loads.append(pltpu.make_async_copy(par_in, par, load_sem.at[8]))
+    loads.append(pltpu.make_async_copy(mom_in, mom, load_sem.at[9]))
     for copy in loads:
         copy.start()
     for k in range(4):
@@ -106,6 +131,22 @@
         copy.wait()
     cot_t[...] = cot[...].astype(F32).T.astype(BF)
 
+    def y_copy(i):
+        return remote(y_out.at[i], y_in.at[i], y_send.at[i], y_recv.at[i], {"outer": 2 * y_at[i] + x_hi})
+
+    def pod_copy():
+        return remote(pod_out, pod_in, pod_send, pod_recv, {"outer": other_hi})
+
+    def v_copy(i):
+        return remote(avg.at[y], avg.at[y], v_send.at[i], v_recv.at[i], {"outer": 2 * y_at[i] + x_hi})
+
+    def pg_quarter(at):
+        return pg[:, pl.ds(pl.multiple_of(at * quarter, quarter), quarter)].astype(BF)
+
+    for i in range(1, Y):
+        y_out[i] = pg_quarter(y_at[i])
+        y_copy(i).start()
+
     def column_part(b):
         part[b] = lax.dot_general(
             cot[...], wfull[b], (((1,), (1,)), ((), ())), preferred_element_type=F32
@@ -139,37 +180,10 @@
             part[b] = (part[b].astype(F32) + sib[slot_of(b)].astype(F32)).astype(BF)
             s_copy(b).start()
 
-    make_part(2 * z)
-    make_part(2 * z + 1)
-    pair_part(2 * z)
-    pair_part(2 * z + 1)
-
-    def ag_step(j, carry):
-        for direction in range(2):
-            ag_copy(j, direction).wait_recv()
-
-            @pl.when(j + 2 < STEPS)
-            def _():
-                ag_copy(j + 2, direction).start()
-
-        here_up = ag_piece(j, 0, z - 1)
-        here_down = ag_piece(j, 1, z + 1)
-        make_part(here_up)
-        make_part(here_down)
-        for at, k in ((1, 0), (3, 1), (4, 2), (6, 3)):
-            @pl.when(j == at)
-            def _():
-                hx_copy(k).wait_recv()
-                hf_copy(k).start()
-        pair_part(here_up)
-        pair_part(here_down)
+    def pair_step(j, carry):
+        pair_part(ag_piece(j, 0, z - 1))
+        pair_part(ag_piece(j, 1, z + 1))
         return carry
-
-    lax.fori_loop(0, STEPS, ag_step, 0)
-
-    for k in range(4):
-        hs_copy(k).wait_recv()
-        hf_copy(k).wait_recv()
 
     def rs_piece(j, direction):
         if direction == 0:
@@ -183,12 +197,74 @@
         )
 
     def token_sum(b):
+        @pl.when(owner_core(b) != c)
+        def _():
+            remote(hid.at[b], hid.at[b], hs_send.at[0], hs_recv.at[b], {"tp": sibling}).wait_recv()
+
         return jnp.dot(cot_t[...], hid[b], preferred_element_type=F32)
 
-    for j in range(2):
+    def rs_start(j):
         for direction in range(2):
             rs_out[direction, j] = token_sum(rs_piece(j, direction)).astype(BF)
             rs_copy(j, direction).start()
+
+    make_part(2 * z)
+    make_part(2 * z + 1)
+
+    def ag_step(j, carry):
+        for direction in range(2):
+            ag_copy(j, direction).wait_recv()
+
+            @pl.when(j + 2 < STEPS)
+            def _():
+                ag_copy(j + 2, direction).start()
+
+        make_part(ag_piece(j, 0, z - 1))
+        make_part(ag_piece(j, 1, z + 1))
+        for at, i in ((1, 0), (3, 1), (4, 2), (6, 3)):
+            @pl.when(j == at)
+            def _():
+                hx_copy(i).wait_recv()
+                hf_copy(i).start()
+
+        @pl.when(j == 1)
+        def _():
+            total = pg_quarter(y).astype(F32)
+            for i in range(1, Y):
+                y_copy(i).wait_recv()
+                total += y_in[i].astype(F32)
+            pod_out[...] = total.astype(BF)
+            pod_copy().start()
+
+        @pl.when(j == 4)
+        def _():
+            pair_part(2 * z)
+            pair_part(2 * z + 1)
+            lax.fori_loop(0, 4, pair_step, 0)
+
+        @pl.when(j == 5)
+        def _():
+            rs_start(0)
+
+        @pl.when(j > 4)
+        def _():
+            pair_step(j - 1, 0)
+
+        return carry
+
+    lax.fori_loop(0, STEPS, ag_step, 0)
+    rs_start(1)
+    pair_step(STEPS - 1, 0)
+
+    pod_copy().wait_recv()
+    avg[y] = ((pod_out[...].astype(F32) + pod_in[...].astype(F32)) / (2 * Y)).astype(BF)
+    for i in range(1, Y):
+        v_copy(i).start()
+
+    def add_keys_values(j):
+        for direction in range(2):
+            b = rs_piece(j, direction)
+            kv_acc[...] += jnp.dot(hid[b], wfull[b], preferred_element_type=F32)
 
     kv_acc[...] = jnp.zeros_like(kv_acc)
 
@@ -198,15 +274,31 @@
             rs_copy(j - 2, direction).wait_recv()
             rs_out[direction, j] = (mine + rs_in[direction, j - 2].astype(F32)).astype(BF)
             rs_copy(j, direction).start()
-        for i in range(3):
-            b = 3 * (j - 2) + i
-            kv_acc[...] += jnp.dot(hid[b], wfull[b], preferred_element_type=F32)
+        add_keys_values(j)
         return carry
 
     lax.fori_loop(2, STEPS, rs_step, 0)
-    kv_stage[...] = (kv_acc[...] + jnp.dot(hid[15], wfull[15], preferred_element_type=F32)).astype(BF)
+    own = [token_sum(2 * z + h) for h in range(2)]
+    for j in range(2):
+        add_keys_values(j)
+    for h in range(2):
+        kv_acc[...] += jnp.dot(hid[2 * z + h], wfull[2 * z + h], preferred_element_type=F32)
+    kv_stage[...] = kv_acc[...].astype(BF)
     stores = [pltpu.make_async_copy(kv_stage, kv_out, store_sem.at[0])]
     stores[0].start()
+
+    for i in range(1, Y):
+        v_copy(i).wait_recv()
+    for i in range(Y):
+        columns = pl.ds(i * quarter, quarter)
+        average = avg[i].astype(F32)
+        new_params, new_momentum = nesterov(average, par[:, columns], mom[:, columns])
+        par[:, columns] = new_params
+        mom[:, columns] = new_momentum
+    stores.append(pltpu.make_async_copy(par, par_out, store_sem.at[7]))
+    stores.append(pltpu.make_async_copy(mom, mom_out, store_sem.at[8]))
+    stores[1].start()
+    stores[2].start()
 
     for k in range(4):
         b = 4 * t + k
@@ -222,7 +314,7 @@
     for direction in range(2):
         rs_copy(6, direction).wait_recv()
     for h in range(2):
-        total = token_sum(2 * z + h) + rs_in[0, 6 - h].astype(F32) + rs_in[1, 5 + h].astype(F32)
+        total = own[h] + rs_in[0, 6 - h].astype(F32) + rs_in[1, 5 + h].astype(F32)
         wg_stage[pl.ds(h * half, half)] = total.T.astype(BF)
         stores.append(
             pltpu.make_async_copy(
@@ -241,26 +333,34 @@
         hf_copy(k).wait_send()
         s_copy(4 * peer + k).wait_send()
         p_copy(4 * sibling + k).wait_send()
-        p_copy(4 * (3 - t) + k).wait_send()
+        p_copy(4 * diagonal + k).wait_send()
+    for i in range(1, Y):
+        y_copy(i).wait_send()
+        v_copy(i).wait_send()
+    pod_copy().wait_send()
     for copy in stores:
         copy.wait()
 
 
-def inner(hidden, weights, cotangent):
+def whole_step(pseudo_grad, params, momentum, hidden, weights, cotangent):
     tokens, width = hidden.shape
     rows, cols = weights.shape
+    slab = params.shape
     half = rows // 2
+    quarter = (slab[0], slab[1] // Y)
     sems = pltpu.SemaphoreType.DMA
     any_spec = pl.BlockSpec(memory_space=pl.ANY)
     return pl.pallas_call(
         kernel,
         out_shape=(
+            jax.ShapeDtypeStruct(slab, F32),
+            jax.ShapeDtypeStruct(slab, F32),
             jax.ShapeDtypeStruct((tokens, cols), BF),
             jax.ShapeDtypeStruct((tokens, width), BF),
             jax.ShapeDtypeStruct((rows, cols), BF),
         ),
-        in_specs=[any_spec] * 3,
-        out_specs=[any_spec] * 3,
+        in_specs=[any_spec] * 6,
+        out_specs=[any_spec] * 5,
         scratch_shapes=[
             pltpu.VMEM((PIECES, tokens, half), BF),
             pltpu.VMEM((PIECES, half, cols), BF),
@@ -275,24 +375,32 @@
             pltpu.VMEM((tokens, cols), BF),
             pltpu.VMEM((4, tokens, half), BF),
             pltpu.VMEM((rows, cols), BF),
-            sems((7,)), sems((7,)),
+            pltpu.VMEM(slab, F32),
+            pltpu.VMEM(slab, F32),
+            pltpu.VMEM(slab, F32),
+            pltpu.VMEM((Y,) + quarter, BF),
+            pltpu.VMEM((Y,) + quarter, BF),
+            pltpu.VMEM(quarter, BF),
+            pltpu.VMEM(quarter, BF),
+            pltpu.VMEM((Y,) + quarter, BF),
+            sems((10,)), sems((9,)),
             sems((2, STEPS)), sems((2, STEPS)), sems((2, STEPS)), sems((2, STEPS)),
-            sems((4,)), sems((4,)), sems((4,)), sems((4,)), sems((4,)), sems((4,)),
+            sems((4,)), sems((4,)), sems((8,)), sems((PIECES,)),
             sems((8,)), sems((8,)), sems((4,)), sems((4,)),
+            sems((Y,)), sems((Y,)), sems((Y,)), sems((Y,)), sems, sems,
         ],
         compiler_params=pltpu.CompilerParams(
             collective_id=0, has_side_effects=True, vmem_limit_bytes=60 * 1024 * 1024
         ),
-        cost_estimate=pl.CostEstimate(flops=7_250_000_000, bytes_accessed=8_000_000, transcendentals=0),
-        name="inner_step",
-    )(hidden, weights, cotangent)
+        cost_estimate=pl.CostEstimate(flops=7_250_000_000, bytes_accessed=12_000_000, transcendentals=0),
+        name="whole_step",
+    )(pseudo_grad, params, momentum, hidden, weights, cotangent)
 
 
 def per_device(pseudo_grad, outer_params, momentum, hidden, kv_weight, kv_cotangent):
-    keys_values, input_grad, weight_grad = inner(hidden[0], kv_weight[0], kv_cotangent[0])
-    pods = lax.axis_size("outer")
-    average = lax.psum(pseudo_grad[0].astype(BF), "outer").astype(F32) / pods
-    new_params, new_momentum = nesterov(average, outer_params, momentum)
+    new_params, new_momentum, keys_values, input_grad, weight_grad = whole_step(
+        pseudo_grad[0], outer_params, momentum, hidden[0], kv_weight[0], kv_cotangent[0]
+    )
     return (new_params, new_momentum, keys_values[None], input_grad[None], weight_grad[None])
 
 

time: 157 us -> 139 us (0.89)
  between operations: 14.1 us -> 0.66 us
  other arithmetic: 4.67 us -> 0 us
  local copies, waits for them, and re-layouts: 3.25 us -> 7.53 us
  Pallas kernels: 135 us -> 131 us
    unnamed x11, local copies, waits for them, and re-layouts: 3.25 us -> 7.53 us
    pallas_call x1, Pallas kernels: 135 us -> 131 us  [whole_step(): pl.pallas_call(kernel, out_shape=(jax.ShapeDtypeStruct(slab, F32), jax.Sh...]
    sub x1 -> x0, other arithmetic: 2.75 us -> none  [nesterov(): params_new = params_old - outer_rate * (average + outer_beta * moment_new)]
    convert_element_type x1 -> x0, other arithmetic: 1.92 us -> none  [per_device(): average = lax.psum(pseudo_grad[0].astype(BF), 'outer').astype(F32) / pods]
  transfers between devices with their start and end apart: 1 -> 0, of which waited for: 0 -> 0; matrix products, arithmetic and copies ran while one was open for 0% -> 0% of each run, Pallas kernels for 86% -> 0%
where the time goes in v2:
time: 139 us
  Pallas kernels  131 us (94%)
  local copies, waits for them, and re-layouts  7.53 us (5%)
    pallas_call x1, Pallas kernels, whole_step(): pl.pallas_call(kernel, out_shape=(jax.ShapeDtypeStruct(slab, F32), jax.Sh...  131 us
    unnamed x11, local copies, waits for them, and re-layouts  7.53 us

profile of v2, /device:TPU:1, one launch (start us, length us, event | category | flops | bytes accessed | tf_op | source)
XLA Modules:
  0.0 139.1 jit_solution(12811882658477614112)
XLA Ops:
  0.6 131.0 %whole_step.1 = (f32[64,3072]{1,0:T(8,128)}, f32[64,3072]{1,0:T(8,128)}, bf16[384,256]{1,0:T(8,128)(2,1)}, bf16[384,3072]{1,0:T(8,128)(2,1)}, bf16[1536,256]{1,0:T(8,128)(2,1)}) custom-call(f32[64,3072]{1,0:T(8,128)} %bitcast.11, f32[64,3072]{1,0:T(8,128)} %par_in.1, f32[64,3072]{1,0:T(8,128)} %mom_in.1, bf16[384,3072]{1,0:T(8,128)(2,1)} %bitcast.10, ...), custom_call_target="tpu_custom_call" | custom-call | flops 7249999872 | bytes 12000000 | tf_op jit(solution)/shard_map/whole_step/pallas_call | solution.py:353
  131.6 0.0 copy-start.2
  131.6 0.0 copy-start
  131.6 2.2 %copy.16 = f32[64,3072]{1,0:T(8,128)} copy(f32[64,3072]{1,0:T(8,128)} %get-tuple-element.20) | data formatting | bytes 1572864
  133.8 2.1 %copy.17 = f32[64,3072]{1,0:T(8,128)} copy(f32[64,3072]{1,0:T(8,128)} %get-tuple-element.21) | data formatting | bytes 1572864
  135.9 0.0 copy-done.2
  135.9 0.7 copy.18
  136.6 0.0 copy-done
  136.6 0.0 copy-start.1
  136.6 1.4 %copy.19 = bf16[1,384,3072]{2,1,0:T(8,128)(2,1)} copy(bf16[1,384,3072]{2,1,0:T(8,128)(2,1)S(1)} %bitcast.7) | data formatting | bytes 4718592
  138.0 0.3 copy-done.1
  138.3 0.9 copy.20
Async XLA Ops:
  131.6 4.3 %copy-start.2 = (bf16[384,256]{1,0:T(8,128)(2,1)S(1)}, bf16[384,256]{1,0:T(8,128)(2,1)}, u32[]{:S(2)}) copy-start(bf16[384,256]{1,0:T(8,128)(2,1)} %get-tuple-element.12) | copy-start | bytes 589828
  131.6 5.0 %copy-start = (bf16[384,3072]{1,0:T(8,128)(2,1)S(1)}, bf16[384,3072]{1,0:T(8,128)(2,1)}, u32[]{:S(2)}) copy-start(bf16[384,3072]{1,0:T(8,128)(2,1)} %get-tuple-element.13) | copy-start | bytes 7077892
  136.6 1.7 %copy-start.1 = (bf16[1536,256]{1,0:T(8,128)(2,1)S(1)}, bf16[1536,256]{1,0:T(8,128)(2,1)}, u32[]{:S(2)}) copy-start(bf16[1536,256]{1,0:T(8,128)(2,1)} %get-tuple-element.14) | copy-start | bytes 2359300

commit v3 on v2

--- a/solution.py
+++ b/solution.py
@@ -26,9 +26,9 @@
 def kernel(
     pg_in, par_in, mom_in, hid_in, w_in, cot_in,
     par_out, mom_out, kv_out, ig_out, wg_out,
-    hid, wfull, cot, cot_t, part, sib, far, rs_out, rs_in, kv_acc, kv_stage, ig_stage, wg_stage,
+    hid, wfull, cot, cot_t, part, sib, far, rs_out, rs_in, kv_acc,
     pg, par, mom, y_out, y_in, pod_out, pod_in, avg,
-    load_sem, store_sem,
+    load_sem,
     ag_send, ag_recv, rs_send, rs_recv,
     hx_send, hx_recv, hs_send, hs_recv,
     p_send, p_recv, s_send, s_recv,
@@ -283,9 +283,7 @@
         add_keys_values(j)
     for h in range(2):
         kv_acc[...] += jnp.dot(hid[2 * z + h], wfull[2 * z + h], preferred_element_type=F32)
-    kv_stage[...] = kv_acc[...].astype(BF)
-    stores = [pltpu.make_async_copy(kv_stage, kv_out, store_sem.at[0])]
-    stores[0].start()
+    kv_out[...] = kv_acc[...].astype(BF)
 
     for i in range(1, Y):
         v_copy(i).wait_recv()
@@ -293,21 +291,15 @@
         columns = pl.ds(i * quarter, quarter)
         average = avg[i].astype(F32)
         new_params, new_momentum = nesterov(average, par[:, columns], mom[:, columns])
-        par[:, columns] = new_params
-        mom[:, columns] = new_momentum
-    stores.append(pltpu.make_async_copy(par, par_out, store_sem.at[7]))
-    stores.append(pltpu.make_async_copy(mom, mom_out, store_sem.at[8]))
-    stores[1].start()
-    stores[2].start()
+        par_out[:, columns] = new_params
+        mom_out[:, columns] = new_momentum
 
     for k in range(4):
         b = 4 * t + k
         p_copy(b).wait_recv()
         s_copy(b).wait_recv()
         total = part[b].astype(F32) + sib[4 * x + k].astype(F32) + far[k].astype(F32)
-        ig_stage[k] = total.astype(BF)
-        stores.append(pltpu.make_async_copy(ig_stage.at[k], ig_out.at[:, pl.ds(k * half, half)], store_sem.at[1 + k]))
-        stores[-1].start()
+        ig_out[:, pl.ds(k * half, half)] = total.astype(BF)
 
     for direction in range(2):
         rs_copy(5, direction).wait_recv()
@@ -315,13 +307,7 @@
         rs_copy(6, direction).wait_recv()
     for h in range(2):
         total = own[h] + rs_in[0, 6 - h].astype(F32) + rs_in[1, 5 + h].astype(F32)
-        wg_stage[pl.ds(h * half, half)] = total.T.astype(BF)
-        stores.append(
-            pltpu.make_async_copy(
-                wg_stage.at[pl.ds(h * half, half)], wg_out.at[pl.ds(h * half, half)], store_sem.at[5 + h]
-            )
-        )
-        stores[-1].start()
+        wg_out[pl.ds(h * half, half)] = total.T.astype(BF)
 
     for j in range(STEPS):
         for direction in range(2):
@@ -338,8 +324,6 @@
         y_copy(i).wait_send()
         v_copy(i).wait_send()
     pod_copy().wait_send()
-    for copy in stores:
-        copy.wait()
 
 
 def whole_step(pseudo_grad, params, momentum, hidden, weights, cotangent):
@@ -353,14 +337,14 @@
     return pl.pallas_call(
         kernel,
         out_shape=(
-            jax.ShapeDtypeStruct(slab, F32),
-            jax.ShapeDtypeStruct(slab, F32),
-            jax.ShapeDtypeStruct((tokens, cols), BF),
-            jax.ShapeDtypeStruct((tokens, width), BF),
-            jax.ShapeDtypeStruct((rows, cols), BF),
+            pltpu.VMEM(slab, F32),
+            pltpu.VMEM(slab, F32),
+            pltpu.VMEM((tokens, cols), BF),
+            pltpu.VMEM((tokens, width), BF),
+            pltpu.VMEM((rows, cols), BF),
         ),
         in_specs=[any_spec] * 6,
-        out_specs=[any_spec] * 5,
+        out_specs=[pl.BlockSpec(memory_space=pltpu.VMEM)] * 5,
         scratch_shapes=[
             pltpu.VMEM((PIECES, tokens, half), BF),
             pltpu.VMEM((PIECES, half, cols), BF),
@@ -372,9 +356,6 @@
             pltpu.VMEM((2, STEPS, cols, half), BF),
             pltpu.VMEM((2, STEPS, cols, half), BF),
             pltpu.VMEM((tokens, cols), F32),
-            pltpu.VMEM((tokens, cols), BF),
-            pltpu.VMEM((4, tokens, half), BF),
-            pltpu.VMEM((rows, cols), BF),
             pltpu.VMEM(slab, F32),
             pltpu.VMEM(slab, F32),
             pltpu.VMEM(slab, F32),
@@ -383,23 +364,49 @@
             pltpu.VMEM(quarter, BF),
             pltpu.VMEM(quarter, BF),
             pltpu.VMEM((Y,) + quarter, BF),
-            sems((10,)), sems((9,)),
+            sems((10,)),
             sems((2, STEPS)), sems((2, STEPS)), sems((2, STEPS)), sems((2, STEPS)),
             sems((4,)), sems((4,)), sems((8,)), sems((PIECES,)),
             sems((8,)), sems((8,)), sems((4,)), sems((4,)),
             sems((Y,)), sems((Y,)), sems((Y,)), sems((Y,)), sems, sems,
         ],
         compiler_params=pltpu.CompilerParams(
-            collective_id=0, has_side_effects=True, vmem_limit_bytes=60 * 1024 * 1024
+            collective_id=0, has_side_effects=True, vmem_limit_bytes=56 * 1024 * 1024
         ),
         cost_estimate=pl.CostEstimate(flops=7_250_000_000, bytes_accessed=12_000_000, transcendentals=0),
         name="whole_step",
     )(pseudo_grad, params, momentum, hidden, weights, cotangent)
 
 
+def store_kernel(*refs):
+    sems = refs[-1]
+    count = (len(refs) - 1) // 2
+    copies = [pltpu.make_async_copy(refs[i], refs[count + i], sems.at[i]) for i in range(count)]
+    for copy in copies:
+        copy.start()
+    for copy in copies:
+        copy.wait()
+
+
+def store(*results):
+    any_spec = pl.BlockSpec(memory_space=pl.ANY)
+    return pl.pallas_call(
+        store_kernel,
+        out_shape=tuple(pltpu.HBM(r.shape, r.dtype) for r in results),
+        in_specs=[pl.BlockSpec(memory_space=pltpu.VMEM)] * len(results),
+        out_specs=[pl.BlockSpec(memory_space=pltpu.HBM)] * len(results),
+        scratch_shapes=[pltpu.SemaphoreType.DMA((len(results),))],
+        compiler_params=pltpu.CompilerParams(vmem_limit_bytes=1024 * 1024),
+        name="store_results",
+    )(*results)
+
+
 def per_device(pseudo_grad, outer_params, momentum, hidden, kv_weight, kv_cotangent):
-    new_params, new_momentum, keys_values, input_grad, weight_grad = whole_step(
-        pseudo_grad[0], outer_params, momentum, hidden[0], kv_weight[0], kv_cotangent[0]
+    new_params, new_momentum, keys_values, input_grad, weight_grad = store(
+        *(
+            pltpu.with_memory_space_constraint(r, pltpu.VMEM)
+            for r in whole_step(pseudo_grad[0], outer_params, momentum, hidden[0], kv_weight[0], kv_cotangent[0])
+        )
     )
     return (new_params, new_momentum, keys_values[None], input_grad[None], weight_grad[None])
 

time: 139 us -> 133 us (0.957)
  local copies, waits for them, and re-layouts: 7.53 us -> 0 us
  Pallas kernels: 131 us -> 133 us
    unnamed x11 -> x0, local copies, waits for them, and re-layouts: 7.53 us -> none
    pallas_call x1 -> x2, Pallas kernels: 131 us -> 133 us  [the longest x1 130 us: whole_step(): pl.pallas_call(kernel, out_shape=(pltpu.VMEM(slab, F32), pltpu.VMEM(slab,...]
where the time goes in v3:
time: 133 us
  Pallas kernels  133 us (100%)
    pallas_call x1, Pallas kernels, whole_step(): pl.pallas_call(kernel, out_shape=(pltpu.VMEM(slab, F32), pltpu.VMEM(slab,...  130 us

profile of v3, /device:TPU:1, one launch (start us, length us, event | category | flops | bytes accessed | tf_op | source)
XLA Modules:
  0.0 133.2 jit_solution(14895157998095139195)
XLA Ops:
  0.6 130.3 %whole_step.1 = (f32[64,3072]{1,0:T(8,128)S(1)}, f32[64,3072]{1,0:T(8,128)S(1)}, bf16[384,256]{1,0:T(8,128)(2,1)S(1)}, bf16[384,3072]{1,0:T(8,128)(2,1)S(1)}, bf16[1536,256]{1,0:T(8,128)(2,1)S(1)}) custom-call(f32[64,3072]{1,0:T(8,128)} %bitcast.9, f32[64,3072]{1,0:T(8,128)} %par_in.1, f32[64,3072]{1,0:T(8,128)} %mom_in.1, bf16[384,3072]{1,0:T(8,128)(2,1)} %bitcast.7, ...), custom_call_target="tpu_custom_call" | custom-call | flops 7249999872 | bytes 12000000 | tf_op jit(solution)/shard_map/whole_step/pallas_call | solution.py:337
  130.9 2.3 %store_results.1 = (f32[64,3072]{1,0:T(8,128)}, f32[64,3072]{1,0:T(8,128)}, bf16[384,256]{1,0:T(8,128)(2,1)}, bf16[384,3072]{1,0:T(8,128)(2,1)}, bf16[1536,256]{1,0:T(8,128)(2,1)}) custom-call(f32[64,3072]{1,0:T(8,128)S(1)} %get-tuple-element.15.refs_0_, f32[64,3072]{1,0:T(8,128)S(1)} %get-tuple-element.16.refs_1_, ...), custom_call_target="tpu_custom_call" | custom-call | tf_op jit(solution)/shard_map/store_results/pallas_call | solution.py:393

commit v4 on v3

--- a/solution.py
+++ b/solution.py
@@ -26,7 +26,7 @@
 def kernel(
     pg_in, par_in, mom_in, hid_in, w_in, cot_in,
     par_out, mom_out, kv_out, ig_out, wg_out,
-    hid, wfull, cot, cot_t, part, sib, far, rs_out, rs_in, kv_acc,
+    hid, wfull, cot, cot_t, part, sib, far, rs_out, rs_in, rs_own, kv_acc,
     pg, par, mom, y_out, y_in, pod_out, pod_in, avg,
     load_sem,
     ag_send, ag_recv, rs_send, rs_recv,
@@ -201,7 +201,7 @@
         def _():
             remote(hid.at[b], hid.at[b], hs_send.at[0], hs_recv.at[b], {"tp": sibling}).wait_recv()
 
-        return jnp.dot(cot_t[...], hid[b], preferred_element_type=F32)
+        return jnp.dot(cot_t[...], hid[b], preferred_element_type=F32).T
 
     def rs_start(j):
         for direction in range(2):
@@ -277,8 +277,27 @@
         add_keys_values(j)
         return carry
 
-    lax.fori_loop(2, STEPS, rs_step, 0)
-    own = [token_sum(2 * z + h) for h in range(2)]
+    lax.fori_loop(2, STEPS - 1, rs_step, 0)
+
+    def last_copy(part_at, direction):
+        rows = pl.ds(part_at * (half // 2), half // 2)
+        return remote(
+            rs_out.at[direction, STEPS - 1, rows], rs_in.at[direction, STEPS - 1, rows],
+            rs_send.at[direction, STEPS - 1 + part_at], rs_recv.at[direction, STEPS - 1 + part_at],
+            {"fsdp": up if direction == 0 else down},
+        )
+
+    mine = [token_sum(rs_piece(STEPS - 1, direction)) for direction in range(2)]
+    for direction in range(2):
+        rs_copy(STEPS - 3, direction).wait_recv()
+        for part_at in range(2):
+            low, high = part_at * (half // 2), (part_at + 1) * (half // 2)
+            total = mine[direction][low:high] + rs_in[direction, STEPS - 3, low:high].astype(F32)
+            rs_out[direction, STEPS - 1, low:high] = total.astype(BF)
+            last_copy(part_at, direction).start()
+    add_keys_values(STEPS - 1)
+    for h in range(2):
+        rs_own[h] = token_sum(2 * z + h)
     for j in range(2):
         add_keys_values(j)
     for h in range(2):
@@ -301,18 +320,11 @@
         total = part[b].astype(F32) + sib[4 * x + k].astype(F32) + far[k].astype(F32)
         ig_out[:, pl.ds(k * half, half)] = total.astype(BF)
 
-    for direction in range(2):
-        rs_copy(5, direction).wait_recv()
-    for direction in range(2):
-        rs_copy(6, direction).wait_recv()
-    for h in range(2):
-        total = own[h] + rs_in[0, 6 - h].astype(F32) + rs_in[1, 5 + h].astype(F32)
-        wg_out[pl.ds(h * half, half)] = total.T.astype(BF)
-
     for j in range(STEPS):
         for direction in range(2):
             ag_copy(j, direction).wait_send()
-            rs_copy(j, direction).wait_send()
+            if j < STEPS - 2:
+                rs_copy(j, direction).wait_send()
     for k in range(4):
         hx_copy(k).wait_send()
         hs_copy(k).wait_send()
@@ -324,6 +336,20 @@
         y_copy(i).wait_send()
         v_copy(i).wait_send()
     pod_copy().wait_send()
+
+    for direction in range(2):
+        rs_copy(STEPS - 2, direction).wait_recv()
+        rs_own[1 - direction] += rs_in[direction, STEPS - 2].astype(F32)
+    for part_at in range(2):
+        for direction in range(2):
+            last_copy(part_at, direction).wait_recv()
+            low, high = part_at * (half // 2), (part_at + 1) * (half // 2)
+            total = rs_own[direction, low:high] + rs_in[direction, STEPS - 1, low:high].astype(F32)
+            wg_out[direction * half + low:direction * half + high] = total.astype(BF)
+    for direction in range(2):
+        rs_copy(STEPS - 2, direction).wait_send()
+        for part_at in range(2):
+            last_copy(part_at, direction).wait_send()
 
 
 def whole_step(pseudo_grad, params, momentum, hidden, weights, cotangent):
@@ -353,8 +379,9 @@
             pltpu.VMEM((PIECES, tokens, half), BF),
             pltpu.VMEM((8, tokens, half), BF),
             pltpu.VMEM((4, tokens, half), BF),
-            pltpu.VMEM((2, STEPS, cols, half), BF),
-            pltpu.VMEM((2, STEPS, cols, half), BF),
+            pltpu.VMEM((2, STEPS, half, cols), BF),
+            pltpu.VMEM((2, STEPS, half, cols), BF),
+            pltpu.VMEM((2, half, cols), F32),
             pltpu.VMEM((tokens, cols), F32),
             pltpu.VMEM(slab, F32),
             pltpu.VMEM(slab, F32),
@@ -365,7 +392,7 @@
             pltpu.VMEM(quarter, BF),
             pltpu.VMEM((Y,) + quarter, BF),
             sems((10,)),
-            sems((2, STEPS)), sems((2, STEPS)), sems((2, STEPS)), sems((2, STEPS)),
+            sems((2, STEPS)), sems((2, STEPS)), sems((2, STEPS + 1)), sems((2, STEPS + 1)),
             sems((4,)), sems((4,)), sems((8,)), sems((PIECES,)),
             sems((8,)), sems((8,)), sems((4,)), sems((4,)),
             sems((Y,)), sems((Y,)), sems((Y,)), sems((Y,)), sems, sems,

time: 133 us -> 132 us (level)
  Pallas kernels: 133 us -> 131 us
where the time goes in v4:
time: 132 us
  Pallas kernels  131 us (99%)
    pallas_call x1, Pallas kernels, whole_step(): pl.pallas_call(kernel, out_shape=(pltpu.VMEM(slab, F32), pltpu.VMEM(slab,...  129 us

profile of v4, /device:TPU:1, one launch (start us, length us, event | category | flops | bytes accessed | tf_op | source)
XLA Modules:
  0.0 132.1 jit_solution(3259384423392218844)
XLA Ops:
  0.6 129.2 %whole_step.1 = (f32[64,3072]{1,0:T(8,128)S(1)}, f32[64,3072]{1,0:T(8,128)S(1)}, bf16[384,256]{1,0:T(8,128)(2,1)S(1)}, bf16[384,3072]{1,0:T(8,128)(2,1)S(1)}, bf16[1536,256]{1,0:T(8,128)(2,1)S(1)}) custom-call(f32[64,3072]{1,0:T(8,128)} %bitcast.9, f32[64,3072]{1,0:T(8,128)} %par_in.1, f32[64,3072]{1,0:T(8,128)} %mom_in.1, bf16[384,3072]{1,0:T(8,128)(2,1)} %bitcast.7, ...), custom_call_target="tpu_custom_call" | custom-call | flops 7249999872 | bytes 12000000 | tf_op jit(solution)/shard_map/whole_step/pallas_call | solution.py:363
  129.8 2.3 %store_results.1 = (f32[64,3072]{1,0:T(8,128)}, f32[64,3072]{1,0:T(8,128)}, bf16[384,256]{1,0:T(8,128)(2,1)}, bf16[384,3072]{1,0:T(8,128)(2,1)}, bf16[1536,256]{1,0:T(8,128)(2,1)}) custom-call(f32[64,3072]{1,0:T(8,128)S(1)} %get-tuple-element.15.refs_0_, f32[64,3072]{1,0:T(8,128)S(1)} %get-tuple-element.16.refs_1_, ...), custom_call_target="tpu_custom_call" | custom-call | tf_op jit(solution)/shard_map/store_results/pallas_call | solution.py:420

commit v5 on v4

--- a/solution.py
+++ b/solution.py
@@ -32,7 +32,7 @@
     ag_send, ag_recv, rs_send, rs_recv,
     hx_send, hx_recv, hs_send, hs_recv,
     p_send, p_recv, s_send, s_recv,
-    y_send, y_recv, v_send, v_recv, pod_send, pod_recv,
+    y_send, y_recv, v_send, v_recv, pod_send, pod_recv, here_sem,
 ):
     o = lax.axis_index("outer")
     z = lax.axis_index("fsdp")
@@ -57,11 +57,19 @@
         )
 
     barrier = pltpu.get_barrier_semaphore()
-    partners = [{"fsdp": up}, {"fsdp": down}, {"tp": sibling}, {"tp": peer}, {"outer": other_hi}]
-    partners += [{"outer": 2 * y_at[i] + x_hi} for i in range(1, Y)]
+    partners = [{"fsdp": up}, {"fsdp": down}, {"tp": sibling}, {"tp": peer}]
     for where in partners:
         pl.semaphore_signal(barrier, inc=1, device_id=where, device_id_type=MESH)
-    pl.semaphore_wait(barrier, len(partners))
+    pods = [other_hi] + [2 * y_at[i] + x_hi for i in range(1, Y)]
+    lower = 0
+    for pod in pods:
+        lower += (pod < o).astype(jnp.int32)
+
+        @pl.when(pod > o)
+        def _():
+            pl.semaphore_signal(barrier, inc=1, device_id={"outer": pod}, device_id_type=MESH)
+
+    pl.semaphore_wait(barrier, len(partners) + lower)
 
     def ring(block):
         return lax.rem(block + 2 * Z, Z)
@@ -143,9 +151,10 @@
     def pg_quarter(at):
         return pg[:, pl.ds(pl.multiple_of(at * quarter, quarter), quarter)].astype(BF)
 
-    for i in range(1, Y):
-        y_out[i] = pg_quarter(y_at[i])
-        y_copy(i).start()
+    for pod in pods:
+        @pl.when(pod < o)
+        def _():
+            pl.semaphore_signal(here_sem, inc=1, device_id={"outer": pod}, device_id_type=MESH)
 
     def column_part(b):
         part[b] = lax.dot_general(
@@ -228,6 +237,16 @@
                 hf_copy(i).start()
 
         @pl.when(j == 1)
+        def _():
+            @pl.when(lower < len(pods))
+            def _():
+                pl.semaphore_wait(here_sem, len(pods) - lower)
+
+            for i in range(1, Y):
+                y_out[i] = pg_quarter(y_at[i])
+                y_copy(i).start()
+
+        @pl.when(j == 3)
         def _():
             total = pg_quarter(y).astype(F32)
             for i in range(1, Y):
@@ -395,7 +414,7 @@
             sems((2, STEPS)), sems((2, STEPS)), sems((2, STEPS + 1)), sems((2, STEPS + 1)),
             sems((4,)), sems((4,)), sems((8,)), sems((PIECES,)),
             sems((8,)), sems((8,)), sems((4,)), sems((4,)),
-            sems((Y,)), sems((Y,)), sems((Y,)), sems((Y,)), sems, sems,
+            sems((Y,)), sems((Y,)), sems((Y,)), sems((Y,)), sems, sems, pltpu.SemaphoreType.REGULAR,
         ],
         compiler_params=pltpu.CompilerParams(
             collective_id=0, has_side_effects=True, vmem_limit_bytes=56 * 1024 * 1024

time: 132 us -> 131 us (level)
    pallas_call x1, Pallas kernels: 129 us -> 127 us  [whole_step(): pl.pallas_call(kernel, out_shape=(pltpu.VMEM(slab, F32), pltpu.VMEM(slab,...]
where the time goes in v5:
time: 131 us; the launch traced here: 130 us
  Pallas kernels  130 us (99%)
    pallas_call x1, Pallas kernels, whole_step(): pl.pallas_call(kernel, out_shape=(pltpu.VMEM(slab, F32), pltpu.VMEM(slab,...  127 us

profile of v5, /device:TPU:1, one launch (start us, length us, event | category | flops | bytes accessed | tf_op | source)
XLA Modules:
  0.0 130.4 jit_solution(8851209051397826783)
XLA Ops:
  0.6 127.5 %whole_step.1 = (f32[64,3072]{1,0:T(8,128)S(1)}, f32[64,3072]{1,0:T(8,128)S(1)}, bf16[384,256]{1,0:T(8,128)(2,1)S(1)}, bf16[384,3072]{1,0:T(8,128)(2,1)S(1)}, bf16[1536,256]{1,0:T(8,128)(2,1)S(1)}) custom-call(f32[64,3072]{1,0:T(8,128)} %bitcast.9, f32[64,3072]{1,0:T(8,128)} %par_in.1, f32[64,3072]{1,0:T(8,128)} %mom_in.1, bf16[384,3072]{1,0:T(8,128)(2,1)} %bitcast.7, ...), custom_call_target="tpu_custom_call" | custom-call | flops 7249999872 | bytes 12000000 | tf_op jit(solution)/shard_map/whole_step/pallas_call | solution.py:382
  128.1 2.3 %store_results.1 = (f32[64,3072]{1,0:T(8,128)}, f32[64,3072]{1,0:T(8,128)}, bf16[384,256]{1,0:T(8,128)(2,1)}, bf16[384,3072]{1,0:T(8,128)(2,1)}, bf16[1536,256]{1,0:T(8,128)(2,1)}) custom-call(f32[64,3072]{1,0:T(8,128)S(1)} %get-tuple-element.15.refs_0_, f32[64,3072]{1,0:T(8,128)S(1)} %get-tuple-element.16.refs_1_, ...), custom_call_target="tpu_custom_call" | custom-call | tf_op jit(solution)/shard_map/store_results/pallas_call | solution.py:439

commit v6 on v5

--- a/solution.py
+++ b/solution.py
@@ -15,6 +15,7 @@
 Y = 4
 PIECES = 16
 STEPS = 7
+SMALL = 128
 
 
 def nesterov(average, params_old, moment_old):
@@ -86,6 +87,21 @@
             {"fsdp": up if direction == 0 else down},
         )
 
+    def ag_last(part_at):
+        rows = pl.ds(part_at * (half - SMALL), SMALL if part_at else half - SMALL)
+        b = ag_piece(STEPS - 1, 0, z)
+        return remote(
+            wfull.at[b, rows], wfull.at[b, rows], ag_send.at[0, STEPS - 1 + part_at], ag_recv.at[0, STEPS - 1 + part_at],
+            {"fsdp": up},
+        )
+
+    def ag_detour():
+        b = ag_piece(STEPS - 2, 1, z + 1)
+        rows = pl.ds(half - SMALL, SMALL)
+        return remote(
+            wfull.at[b, rows], wfull.at[b, rows], ag_send.at[1, STEPS], ag_recv.at[0, STEPS], {"fsdp": down}
+        )
+
     def ag_first(j, direction):
         h = j if direction == 0 else 1 - j
         return remote(
@@ -221,12 +237,36 @@
     make_part(2 * z + 1)
 
     def ag_step(j, carry):
-        for direction in range(2):
-            ag_copy(j, direction).wait_recv()
-
-            @pl.when(j + 2 < STEPS)
+        @pl.when(j < STEPS - 1)
+        def _():
+            ag_copy(j, 0).wait_recv()
+
+        @pl.when(j == STEPS - 1)
+        def _():
+            ag_last(0).wait_recv()
+            ag_last(1).wait_recv()
+
+        @pl.when(j + 2 < STEPS - 1)
+        def _():
+            ag_copy(j + 2, 0).start()
+
+        @pl.when(j + 2 == STEPS - 1)
+        def _():
+            ag_last(0).start()
+
+            @pl.when(z != Z - 1)
             def _():
-                ag_copy(j + 2, direction).start()
+                ag_last(1).start()
+
+        ag_copy(j, 1).wait_recv()
+
+        @pl.when(j + 2 < STEPS)
+        def _():
+            ag_copy(j + 2, 1).start()
+
+        @pl.when((j == STEPS - 2) & (z == 1))
+        def _():
+            ag_detour().start()
 
         make_part(ag_piece(j, 0, z - 1))
         make_part(ag_piece(j, 1, z + 1))
@@ -339,9 +379,20 @@
         total = part[b].astype(F32) + sib[4 * x + k].astype(F32) + far[k].astype(F32)
         ig_out[:, pl.ds(k * half, half)] = total.astype(BF)
 
+    ag_last(0).wait_send()
+
+    @pl.when(z != Z - 1)
+    def _():
+        ag_last(1).wait_send()
+
+    @pl.when(z == 1)
+    def _():
+        ag_detour().wait_send()
+
     for j in range(STEPS):
         for direction in range(2):
-            ag_copy(j, direction).wait_send()
+            if j < STEPS - 1 or direction == 1:
+                ag_copy(j, direction).wait_send()
             if j < STEPS - 2:
                 rs_copy(j, direction).wait_send()
     for k in range(4):
@@ -411,7 +462,7 @@
             pltpu.VMEM(quarter, BF),
             pltpu.VMEM((Y,) + quarter, BF),
             sems((10,)),
-            sems((2, STEPS)), sems((2, STEPS)), sems((2, STEPS + 1)), sems((2, STEPS + 1)),
+            sems((2, STEPS + 1)), sems((2, STEPS + 1)), sems((2, STEPS + 1)), sems((2, STEPS + 1)),
             sems((4,)), sems((4,)), sems((8,)), sems((PIECES,)),
             sems((8,)), sems((8,)), sems((4,)), sems((4,)),
             sems((Y,)), sems((Y,)), sems((Y,)), sems((Y,)), sems, sems, pltpu.SemaphoreType.REGULAR,

time: 131 us -> 130 us (level)
  no operation moved by 1% of the time
where the time goes in v6:
time: 130 us; the launch traced here: 129 us
  Pallas kernels  129 us (99%)
    pallas_call x1, Pallas kernels, whole_step(): pl.pallas_call(kernel, out_shape=(pltpu.VMEM(slab, F32), pltpu.VMEM(slab,...  126 us

profile of v6, /device:TPU:1, one launch (start us, length us, event | category | flops | bytes accessed | tf_op | source)
XLA Modules:
  0.0 129.4 jit_solution(10215808934617074163)
XLA Ops:
  0.6 126.5 %whole_step.1 = (f32[64,3072]{1,0:T(8,128)S(1)}, f32[64,3072]{1,0:T(8,128)S(1)}, bf16[384,256]{1,0:T(8,128)(2,1)S(1)}, bf16[384,3072]{1,0:T(8,128)(2,1)S(1)}, bf16[1536,256]{1,0:T(8,128)(2,1)S(1)}) custom-call(f32[64,3072]{1,0:T(8,128)} %bitcast.9, f32[64,3072]{1,0:T(8,128)} %par_in.1, f32[64,3072]{1,0:T(8,128)} %mom_in.1, bf16[384,3072]{1,0:T(8,128)(2,1)} %bitcast.7, ...), custom_call_target="tpu_custom_call" | custom-call | flops 7249999872 | bytes 12000000 | tf_op jit(solution)/shard_map/whole_step/pallas_call | solution.py:433
  127.1 2.3 %store_results.1 = (f32[64,3072]{1,0:T(8,128)}, f32[64,3072]{1,0:T(8,128)}, bf16[384,256]{1,0:T(8,128)(2,1)}, bf16[384,3072]{1,0:T(8,128)(2,1)}, bf16[1536,256]{1,0:T(8,128)(2,1)}) custom-call(f32[64,3072]{1,0:T(8,128)S(1)} %get-tuple-element.15.refs_0_, f32[64,3072]{1,0:T(8,128)S(1)} %get-tuple-element.16.refs_1_, ...), custom_call_target="tpu_custom_call" | custom-call | tf_op jit(solution)/shard_map/store_results/pallas_call | solution.py:490

commit v7 on v6

--- a/solution.py
+++ b/solution.py
@@ -70,75 +70,9 @@
         def _():
             pl.semaphore_signal(barrier, inc=1, device_id={"outer": pod}, device_id_type=MESH)
 
-    pl.semaphore_wait(barrier, len(partners) + lower)
-
-    def ring(block):
-        return lax.rem(block + 2 * Z, Z)
-
-    def ag_piece(j, direction, at):
-        if direction == 0:
-            return 2 * ring(at - j // 2) + lax.rem(j, 2)
-        return 2 * ring(at + j // 2) + 1 - lax.rem(j, 2)
-
-    def ag_copy(j, direction):
-        b = ag_piece(j, direction, z)
-        return remote(
-            wfull.at[b], wfull.at[b], ag_send.at[direction, j], ag_recv.at[direction, j],
-            {"fsdp": up if direction == 0 else down},
-        )
-
-    def ag_last(part_at):
-        rows = pl.ds(part_at * (half - SMALL), SMALL if part_at else half - SMALL)
-        b = ag_piece(STEPS - 1, 0, z)
-        return remote(
-            wfull.at[b, rows], wfull.at[b, rows], ag_send.at[0, STEPS - 1 + part_at], ag_recv.at[0, STEPS - 1 + part_at],
-            {"fsdp": up},
-        )
-
-    def ag_detour():
-        b = ag_piece(STEPS - 2, 1, z + 1)
-        rows = pl.ds(half - SMALL, SMALL)
-        return remote(
-            wfull.at[b, rows], wfull.at[b, rows], ag_send.at[1, STEPS], ag_recv.at[0, STEPS], {"fsdp": down}
-        )
-
-    def ag_first(j, direction):
-        h = j if direction == 0 else 1 - j
-        return remote(
-            w_in.at[pl.ds(h * half, half)], wfull.at[2 * z + h], ag_send.at[direction, j], ag_recv.at[direction, j],
-            {"fsdp": up if direction == 0 else down},
-        )
-
-    for j in range(2):
-        for direction in range(2):
-            ag_first(j, direction).start()
-
-    def farther(of):
-        low = ring(2 * of - z)
-        high = ring(2 * of + 1 - z)
-        return (jnp.minimum(high, Z - high) > jnp.minimum(low, Z - low)).astype(jnp.int32)
-
-    def hid_turn(i, of):
-        first = farther(of)
-        return 2 * lax.rem(first + i // 2, 2) + i % 2
-
     def hid_view(k):
         return hid_in.at[:, pl.ds(pl.multiple_of(k * half, half), half)]
 
-    def hx_copy(i):
-        k = hid_turn(i, t)
-        return remote(hid_view(k), hid.at[4 * t + k], hx_send.at[i], hx_recv.at[i], {"tp": peer})
-
-    def hs_copy(k):
-        b = 4 * t + k
-        return remote(hid_view(k), hid.at[b], hs_send.at[k], hs_recv.at[b], {"tp": sibling})
-
-    def hf_copy(i):
-        b = 4 * peer + hid_turn(i, peer)
-        return remote(hid.at[b], hid.at[b], hs_send.at[4 + i], hs_recv.at[b], {"tp": sibling})
-
-    for i in range(4):
-        hx_copy(i).start()
     loads = [pltpu.make_async_copy(cot_in, cot, load_sem.at[0])]
     for h in range(2):
         loads.append(pltpu.make_async_copy(w_in.at[pl.ds(h * half, half)], wfull.at[2 * z + h], load_sem.at[1 + h]))
@@ -149,6 +83,73 @@
     loads.append(pltpu.make_async_copy(mom_in, mom, load_sem.at[9]))
     for copy in loads:
         copy.start()
+
+    pl.semaphore_wait(barrier, len(partners) + lower)
+
+    def ring(block):
+        return lax.rem(block + 2 * Z, Z)
+
+    def ag_piece(j, direction, at):
+        if direction == 0:
+            return 2 * ring(at - j // 2) + lax.rem(j, 2)
+        return 2 * ring(at + j // 2) + 1 - lax.rem(j, 2)
+
+    def ag_copy(j, direction):
+        b = ag_piece(j, direction, z)
+        return remote(
+            wfull.at[b], wfull.at[b], ag_send.at[direction, j], ag_recv.at[direction, j],
+            {"fsdp": up if direction == 0 else down},
+        )
+
+    def ag_last(part_at):
+        rows = pl.ds(part_at * (half - SMALL), SMALL if part_at else half - SMALL)
+        b = ag_piece(STEPS - 1, 0, z)
+        return remote(
+            wfull.at[b, rows], wfull.at[b, rows], ag_send.at[0, STEPS - 1 + part_at], ag_recv.at[0, STEPS - 1 + part_at],
+            {"fsdp": up},
+        )
+
+    def ag_detour():
+        b = ag_piece(STEPS - 2, 1, z + 1)
+        rows = pl.ds(half - SMALL, SMALL)
+        return remote(
+            wfull.at[b, rows], wfull.at[b, rows], ag_send.at[1, STEPS], ag_recv.at[0, STEPS], {"fsdp": down}
+        )
+
+    def ag_first(j, direction):
+        h = j if direction == 0 else 1 - j
+        return remote(
+            w_in.at[pl.ds(h * half, half)], wfull.at[2 * z + h], ag_send.at[direction, j], ag_recv.at[direction, j],
+            {"fsdp": up if direction == 0 else down},
+        )
+
+    for j in range(2):
+        for direction in range(2):
+            ag_first(j, direction).start()
+
+    def farther(of):
+        low = ring(2 * of - z)
+        high = ring(2 * of + 1 - z)
+        return (jnp.minimum(high, Z - high) > jnp.minimum(low, Z - low)).astype(jnp.int32)
+
+    def hid_turn(i, of):
+        first = farther(of)
+        return 2 * lax.rem(first + i // 2, 2) + i % 2
+
+    def hx_copy(i):
+        k = hid_turn(i, t)
+        return remote(hid_view(k), hid.at[4 * t + k], hx_send.at[i], hx_recv.at[i], {"tp": peer})
+
+    def hs_copy(k):
+        b = 4 * t + k
+        return remote(hid_view(k), hid.at[b], hs_send.at[k], hs_recv.at[b], {"tp": sibling})
+
+    def hf_copy(i):
+        b = 4 * peer + hid_turn(i, peer)
+        return remote(hid.at[b], hid.at[b], hs_send.at[4 + i], hs_recv.at[b], {"tp": sibling})
+
+    for i in range(4):
+        hx_copy(i).start()
     for k in range(4):
         hs_copy(k).start()
     for copy in loads:

time: 130 us -> 130 us (level)
  no operation moved by 1% of the time
where the time goes in v7:
time: 130 us; the launch traced here: 129 us
  Pallas kernels  129 us (99%)
    pallas_call x1, Pallas kernels, whole_step(): pl.pallas_call(kernel, out_shape=(pltpu.VMEM(slab, F32), pltpu.VMEM(slab,...  126 us

profile of v7, /device:TPU:1, one launch (start us, length us, event | category | flops | bytes accessed | tf_op | source)
XLA Modules:
  0.0 129.4 jit_solution(17415504528820500024)
XLA Ops:
  0.6 126.5 %whole_step.1 = (f32[64,3072]{1,0:T(8,128)S(1)}, f32[64,3072]{1,0:T(8,128)S(1)}, bf16[384,256]{1,0:T(8,128)(2,1)S(1)}, bf16[384,3072]{1,0:T(8,128)(2,1)S(1)}, bf16[1536,256]{1,0:T(8,128)(2,1)S(1)}) custom-call(f32[64,3072]{1,0:T(8,128)} %bitcast.9, f32[64,3072]{1,0:T(8,128)} %par_in.1, f32[64,3072]{1,0:T(8,128)} %mom_in.1, bf16[384,3072]{1,0:T(8,128)(2,1)} %bitcast.7, ...), custom_call_target="tpu_custom_call" | custom-call | flops 7249999872 | bytes 12000000 | tf_op jit(solution)/shard_map/whole_step/pallas_call | solution.py:434
  127.1 2.3 %store_results.1 = (f32[64,3072]{1,0:T(8,128)}, f32[64,3072]{1,0:T(8,128)}, bf16[384,256]{1,0:T(8,128)(2,1)}, bf16[384,3072]{1,0:T(8,128)(2,1)}, bf16[1536,256]{1,0:T(8,128)(2,1)}) custom-call(f32[64,3072]{1,0:T(8,128)S(1)} %get-tuple-element.15.refs_0_, f32[64,3072]{1,0:T(8,128)S(1)} %get-tuple-element.16.refs_1_, ...), custom_call_target="tpu_custom_call" | custom-call | tf_op jit(solution)/shard_map/store_results/pallas_call | solution.py:491
